TPU v7x, 32 devices: a whole 2x2x4 slice. The times are simulated.
32 devices in a mesh: row: 8 (over z, core), col: 4 (over y, x).
Axes of the slice: x: 2, y: 2, z: 4, core: 2. Of those that a mesh axis runs over, the one named last changes fastest.
Arguments:
- a_blocks: bfloat16 [8, 4, 32, 128, 128], P('row', 'col'), may hold values from -6 to 6
- a_coord: int32 [8, 4, 32, 2], P('row', 'col'), may hold values from -1 to 31, as said below
- b_blocks: bfloat16 [8, 4, 32, 128, 128], P('row', 'col'), may hold values from -0.125 to 0.125
- b_coord: int32 [8, 4, 32, 2], P('row', 'col'), may hold values from -1 to 31, as said below
- c_mask: int32 [32, 32], P('row', 'col'), may hold values 0 or 1
Outputs:
- c_blocks: float32 [4096, 4096], P('row', 'col')
Inputs may be any that keep to these rules, and one draw needn't show every extreme that they name: `a_coord`: entry [i, s, t] holds the block row and block column of the block in slot t of device (i, s), or -1 in both for an empty slot. Its block row lies in i * 4 to (i + 1) * 4 - 1. With p = column // 4, slot t lies in t // 8 = (p - i) mod 4. No block is named twice. `b_coord`: entry [s, j, t] holds the block row and block column of the block in slot t of device (s, j), or -1 in both for an empty slot. Its block column lies in j * 8 to (j + 1) * 8 - 1. With p = row // 4, slot t lies in t // 4 = (p - j) mod 8. No block is named twice.
All inputs are finite; a program needn't handle non-finite values. No bound on the sum of `c_mask` on one device may be relied on, other than what follows from the above.
Results may differ from a plain program's by a relative error of at most 0.0003.
Values may be sent and summed in bfloat16 or wider, within the bound.
A program may use at most 64 MiB of HBM per device.

v0:
```python
import jax
import jax.numpy as jnp
from jax import lax
from jax.sharding import PartitionSpec as P


def passed_along(value, axis, steps):
    count = lax.axis_size(axis)
    pairs = [(source, (source + steps) % count) for source in range(count)]
    return lax.ppermute(value, axis, pairs)


def roll_panel(panel_b):
    return passed_along(panel_b, "row", -1)


def shards(a_blocks, a_coord, b_blocks, b_coord, c_mask):
    row_count = lax.axis_size("row")
    col_count = lax.axis_size("col")
    panel_ratio = row_count // col_count
    grid_row = lax.axis_index("row")
    grid_col = lax.axis_index("col")
    block_size = a_blocks.shape[-1]
    band_rows = c_mask.shape[0]
    band_cols = c_mask.shape[1]
    a_send = a_blocks.reshape(col_count, -1, block_size, block_size)
    a_tags = a_coord.reshape(col_count, -1, 2)
    a_recv, a_tags = (
        lax.all_to_all(a_send, "col", split_axis=0, concat_axis=0, tiled=True),
        lax.all_to_all(a_tags, "col", split_axis=0, concat_axis=0, tiled=True),
    )
    a_recv = a_recv.reshape(-1, block_size, block_size)
    a_tags = a_tags.reshape(-1, 2)
    a_live = a_tags[:, 0] >= 0
    panel_index = a_tags[:, 1] // band_rows
    count_a = panel_ratio * band_rows * band_rows
    a_pos = (
        panel_index // col_count * band_rows * band_rows
        + (a_tags[:, 0] - grid_row * band_rows) * band_rows
        + a_tags[:, 1] % band_rows
    )
    a_pos = jnp.where(a_live, a_pos, count_a)
    a_tile = (
        jnp.zeros((count_a, block_size, block_size), a_blocks.dtype)
        .at[a_pos]
        .set(a_recv, mode="drop")
    )
    a_group = a_tile.reshape(panel_ratio, band_rows, band_rows, block_size, block_size)
    a_group = a_group.transpose(0, 1, 3, 2, 4).reshape(
        panel_ratio, band_rows * block_size, band_rows * block_size
    )
    b_send = b_blocks.reshape(row_count, -1, block_size, block_size)
    b_tags = b_coord.reshape(row_count, -1, 2)
    b_recv, b_tags = (
        lax.all_to_all(b_send, "row", split_axis=0, concat_axis=0, tiled=True),
        lax.all_to_all(b_tags, "row", split_axis=0, concat_axis=0, tiled=True),
    )
    b_recv = b_recv.reshape(-1, block_size, block_size)
    b_tags = b_tags.reshape(-1, 2)
    b_live = b_tags[:, 0] >= 0
    count_b = band_rows * band_cols
    b_pos = b_tags[:, 0] % band_rows * band_cols + b_tags[:, 1] - grid_col * band_cols
    b_pos = jnp.where(b_live, b_pos, count_b)
    b_tile = (
        jnp.zeros((count_b, block_size, block_size), b_blocks.dtype)
        .at[b_pos]
        .set(b_recv, mode="drop")
    )
    b_panel = b_tile.reshape(band_rows, band_cols, block_size, block_size)
    b_panel = b_panel.transpose(0, 2, 1, 3).reshape(band_rows * block_size, band_cols * block_size)
    offset = grid_row + grid_col
    accumulated = jnp.zeros((band_rows * block_size, band_cols * block_size), jnp.float32)

    def advance(step_index, carried):
        a_current, panel_b, running = carried
        member = (offset + step_index) % row_count // col_count
        a_use = lax.dynamic_index_in_dim(a_current, member, 0, keepdims=False)
        running = running + jnp.dot(a_use, panel_b, preferred_element_type=jnp.float32)
        a_current = passed_along(a_current, "col", -1)
        return (a_current, roll_panel(panel_b), running)

    a_last, b_last, accumulated = lax.fori_loop(
        0, row_count - 1, advance, (a_group, b_panel, accumulated)
    )
    member = (offset + row_count - 1) % row_count // col_count
    a_use = lax.dynamic_index_in_dim(a_last, member, 0, keepdims=False)
    accumulated = accumulated + jnp.dot(a_use, b_last, preferred_element_type=jnp.float32)
    masked = accumulated.reshape(band_rows, block_size, band_cols, block_size) * c_mask[
        :, None, :, None
    ].astype(jnp.float32)
    return masked.reshape(band_rows * block_size, band_cols * block_size)


def solution(mesh):
    placed = (
        P("row", "col", None, None, None),
        P("row", "col", None, None),
        P("row", "col", None, None, None),
        P("row", "col", None, None),
        P("row", "col"),
    )
    return jax.shard_map(
        shards, mesh=mesh, in_specs=placed, out_specs=P("row", "col"), check_vma=False
    )
```

profile of v0, /device:TPU:0, one launch (start us, length us, event | category | flops | bytes accessed | tf_op | source)
XLA Modules:
  0.0 258.3 jit_solution(16308488505931294219)
XLA Ops:
  1.4 5.2 %all-to-all-start = ((s32[4,8,2]{1,2,0:T(2,128)}), s32[4,8,2]{1,2,0:T(2,128)S(1)}, u32[]{:S(2)}, u32[]{:S(2)}) async-start(s32[4,8,2]{1,2,0:T(2,128)} %copy.8), calls=%async_computation | async-start | bytes 8192 | tf_op jit(solution)/shard_map/all_to_all | solution.py:30
  7.3 3.9 %all-to-all-done = s32[4,8,2]{1,2,0:T(2,128)S(1)} async-done(((s32[4,8,2]{1,2,0:T(2,128)}), s32[4,8,2]{1,2,0:T(2,128)S(1)}, u32[]{:S(2)}, u32[]{:S(2)}) %all-to-all-start) | async-done | bytes 288 | tf_op jit(solution)/shard_map/all_to_all | solution.py:30
  11.2 10.3 %all_to_all.20 = s32[8,4,2]{1,2,0:T(2,128)S(1)} all-to-all(s32[8,4,2]{1,2,0:T(2,128)S(1)} %copy.11), channel_id=1, replica_groups=mesh['row'=8,'col'=4] {'row'}, dimensions={0} | all-to-all | bytes 512 | tf_op jit(solution)/shard_map/all_to_all | solution.py:56
  21.5 18.8 %all_to_all.21 = bf16[4,8,128,128]{3,2,1,0:T(8,128)(2,1)} all-to-all(bf16[4,8,128,128]{3,2,1,0:T(8,128)(2,1)} %bitcast.48), channel_id=1, replica_groups=mesh['row'=8,'col'=4] {'col'}, dimensions={0} | all-to-all | bytes 2097152 | tf_op jit(solution)/shard_map/all_to_all | solution.py:29
  40.3 4.2 %all-to-all-start.3 = ((bf16[8,4,128,128]{3,2,1,0:T(8,128)(2,1)}), bf16[8,4,128,128]{3,2,1,0:T(8,128)(2,1)}, u32[]{:S(2)}, u32[]{:S(2)}) async-start(bf16[8,4,128,128]{3,2,1,0:T(8,128)(2,1)} %bitcast.6), calls=%async_computation.3 | async-start | bytes 2097152 | tf_op jit(solution)/shard_map/all_to_all | solution.py:55
  45.1 3.6 %scatter_fusion = bf16[32,128,128]{2,1,0:T(8,128)(2,1)S(1)} fusion(bf16[32,128,128]{2,1,0:T(8,128)(2,1)S(1)} %broadcast.69.clone, s32[32]{0:T(128)S(1)} %fusion.9, bf16[32,128,128]{2,1,0:T(8,128)(2,1)} %bitcast.46), kind=kCustom, calls=%fused_computation | custom fusion | bytes 3145856 | tf_op jit(solution)/shard_map/scatter | solution.py:46
  52.7 18.4 %all-to-all-done.3 = bf16[8,4,128,128]{3,2,1,0:T(8,128)(2,1)} async-done(((bf16[8,4,128,128]{3,2,1,0:T(8,128)(2,1)}), bf16[8,4,128,128]{3,2,1,0:T(8,128)(2,1)}, u32[]{:S(2)}, u32[]{:S(2)}) %all-to-all-start.3) | async-done | bytes 1048608 | tf_op jit(solution)/shard_map/all_to_all | solution.py:55
  71.4 3.6 %scatter_fusion.1 = bf16[32,128,128]{2,1,0:T(8,128)(2,1)S(1)} fusion(bf16[32,128,128]{2,1,0:T(8,128)(2,1)S(1)} %broadcast.69.clone.1, s32[32]{0:T(128)S(1)} %fusion.10, bf16[32,128,128]{2,1,0:T(8,128)(2,1)} %bitcast.7), kind=kCustom, calls=%fused_computation.1 | custom fusion | bytes 3145856 | tf_op jit(solution)/shard_map/scatter | solution.py:67
  76.9 177.6 %while.20 = (s32[]{:T(128)}, bf16[2,512,512]{2,1,0:T(8,128)(2,1)}, bf16[512,1024]{1,0:T(8,128)(2,1)}, f32[512,1024]{1,0:T(8,128)S(1)}, s32[]{:T(128)}, /*index=5...) while((s32[]{:T(128)}, bf16[2,512,512]{2,1,0:T(8,128)(2,1)}, ...), condition=%wide.region_3.4_spmd.clone, body=%wide.region_2.3_spmd.clone.sunk | while | flops 537919488 | bytes 18350596 | solution.py:82
  84.0 20.2 %collective-permute-done = bf16[2,512,512]{2,1,0:T(8,128)(2,1)} collective-permute-done((bf16[2,512,512]{2,1,0:T(8,128)(2,1)}, bf16[2,512,512]{2,1,0:T(8,128)(2,1)}, u32[]{:S(2)}, u32[]{:S(2)}) %collective-permute-start) | collective-permute-done | bytes 1048608 | tf_op jit(solution)/shard_map/while/body/eval_jaxpr/ppermute | solution.py:10
  104.2 2.3 copy.26
  111.8 18.9 %collective-permute-done = bf16[2,512,512]{2,1,0:T(8,128)(2,1)} collective-permute-done((bf16[2,512,512]{2,1,0:T(8,128)(2,1)}, bf16[2,512,512]{2,1,0:T(8,128)(2,1)}, u32[]{:S(2)}, u32[]{:S(2)}) %collective-permute-start) | collective-permute-done | bytes 1048608 | tf_op jit(solution)/shard_map/while/body/eval_jaxpr/ppermute | solution.py:10
  132.9 2.6 %collective-permute-start = (bf16[2,512,512]{2,1,0:T(8,128)(2,1)}, bf16[2,512,512]{2,1,0:T(8,128)(2,1)}, u32[]{:S(2)}, u32[]{:S(2)}) collective-permute-start(bf16[2,512,512]{2,1,0:T(8,128)(2,1)} %copy.26), channel_id=1, source_target_pairs={{0,3},{1,0},{2,1},{3,2},{4,7},{5,4},{6,5},{7,6},{8,11},{9,8},{10,9... | collective-permute-start | bytes 3145736 | tf_op jit(solution)/shard_map/while/body/eval_jaxpr/ppermute | solution.py:10
  138.9 18.2 %collective-permute-done = bf16[2,512,512]{2,1,0:T(8,128)(2,1)} collective-permute-done((bf16[2,512,512]{2,1,0:T(8,128)(2,1)}, bf16[2,512,512]{2,1,0:T(8,128)(2,1)}, u32[]{:S(2)}, u32[]{:S(2)}) %collective-permute-start) | collective-permute-done | bytes 1048608 | tf_op jit(solution)/shard_map/while/body/eval_jaxpr/ppermute | solution.py:10
  157.0 2.3 copy.26
  159.3 2.6 %collective-permute-start = (bf16[2,512,512]{2,1,0:T(8,128)(2,1)}, bf16[2,512,512]{2,1,0:T(8,128)(2,1)}, u32[]{:S(2)}, u32[]{:S(2)}) collective-permute-start(bf16[2,512,512]{2,1,0:T(8,128)(2,1)} %copy.26), channel_id=1, source_target_pairs={{0,3},{1,0},{2,1},{3,2},{4,7},{5,4},{6,5},{7,6},{8,11},{9,8},{10,9... | collective-permute-start | bytes 3145736 | tf_op jit(solution)/shard_map/while/body/eval_jaxpr/ppermute | solution.py:10
  165.2 17.2 %collective-permute-done = bf16[2,512,512]{2,1,0:T(8,128)(2,1)} collective-permute-done((bf16[2,512,512]{2,1,0:T(8,128)(2,1)}, bf16[2,512,512]{2,1,0:T(8,128)(2,1)}, u32[]{:S(2)}, u32[]{:S(2)}) %collective-permute-start) | collective-permute-done | bytes 1048608 | tf_op jit(solution)/shard_map/while/body/eval_jaxpr/ppermute | solution.py:10
  184.7 2.6 %collective-permute-start = (bf16[2,512,512]{2,1,0:T(8,128)(2,1)}, bf16[2,512,512]{2,1,0:T(8,128)(2,1)}, u32[]{:S(2)}, u32[]{:S(2)}) collective-permute-start(bf16[2,512,512]{2,1,0:T(8,128)(2,1)} %copy.26), channel_id=1, source_target_pairs={{0,3},{1,0},{2,1},{3,2},{4,7},{5,4},{6,5},{7,6},{8,11},{9,8},{10,9... | collective-permute-start | bytes 3145736 | tf_op jit(solution)/shard_map/while/body/eval_jaxpr/ppermute | solution.py:10
  190.7 16.3 %collective-permute-done = bf16[2,512,512]{2,1,0:T(8,128)(2,1)} collective-permute-done((bf16[2,512,512]{2,1,0:T(8,128)(2,1)}, bf16[2,512,512]{2,1,0:T(8,128)(2,1)}, u32[]{:S(2)}, u32[]{:S(2)}) %collective-permute-start) | collective-permute-done | bytes 1048608 | tf_op jit(solution)/shard_map/while/body/eval_jaxpr/ppermute | solution.py:10
  209.3 2.6 %collective-permute-start = (bf16[2,512,512]{2,1,0:T(8,128)(2,1)}, bf16[2,512,512]{2,1,0:T(8,128)(2,1)}, u32[]{:S(2)}, u32[]{:S(2)}) collective-permute-start(bf16[2,512,512]{2,1,0:T(8,128)(2,1)} %copy.26), channel_id=1, source_target_pairs={{0,3},{1,0},{2,1},{3,2},{4,7},{5,4},{6,5},{7,6},{8,11},{9,8},{10,9... | collective-permute-start | bytes 3145736 | tf_op jit(solution)/shard_map/while/body/eval_jaxpr/ppermute | solution.py:10
  215.2 15.4 %collective-permute-done = bf16[2,512,512]{2,1,0:T(8,128)(2,1)} collective-permute-done((bf16[2,512,512]{2,1,0:T(8,128)(2,1)}, bf16[2,512,512]{2,1,0:T(8,128)(2,1)}, u32[]{:S(2)}, u32[]{:S(2)}) %collective-permute-start) | collective-permute-done | bytes 1048608 | tf_op jit(solution)/shard_map/while/body/eval_jaxpr/ppermute | solution.py:10
  232.9 2.6 %collective-permute-start = (bf16[2,512,512]{2,1,0:T(8,128)(2,1)}, bf16[2,512,512]{2,1,0:T(8,128)(2,1)}, u32[]{:S(2)}, u32[]{:S(2)}) collective-permute-start(bf16[2,512,512]{2,1,0:T(8,128)(2,1)} %copy.26), channel_id=1, source_target_pairs={{0,3},{1,0},{2,1},{3,2},{4,7},{5,4},{6,5},{7,6},{8,11},{9,8},{10,9... | collective-permute-start | bytes 3145736 | tf_op jit(solution)/shard_map/while/body/eval_jaxpr/ppermute | solution.py:10
  238.8 15.7 %collective-permute-done = bf16[2,512,512]{2,1,0:T(8,128)(2,1)} collective-permute-done((bf16[2,512,512]{2,1,0:T(8,128)(2,1)}, bf16[2,512,512]{2,1,0:T(8,128)(2,1)}, u32[]{:S(2)}, u32[]{:S(2)}) %collective-permute-start) | collective-permute-done | bytes 1048608 | tf_op jit(solution)/shard_map/while/body/eval_jaxpr/ppermute | solution.py:10
  254.7 3.6 %bitcast_multiply_fusion = f32[512,1024]{1,0:T(8,128)} fusion(f32[64,8,8,128]{3,2,1,0:T(8,128)S(1)} %bitcast.45, f32[512,1024]{1,0:T(8,128)S(1)} %get-tuple-element.142, bf16[512,1024]{1,0:T(8,128)(2,1)} %get-tuple-element.144, bf16[2,512,512]{2,1,0:T(8,128)(2,1)} %get-tuple-element.143, s32[]{:T(128)S(6)} %select_n.101), kind=kOutput, calls=%fused_computation.6 | convolution fusion | flops 537919488 | bytes 7864324 | tf_op jit(solution)/shard_map/dot_general | solution.py:87
  (56 shorter events, 46.9 us)
Async XLA Ops:
  1.4 9.8 %all-to-all-start = ((s32[4,8,2]{1,2,0:T(2,128)}), s32[4,8,2]{1,2,0:T(2,128)S(1)}, u32[]{:S(2)}, u32[]{:S(2)}) async-start(s32[4,8,2]{1,2,0:T(2,128)} %copy.8), calls=%async_computation | async-start | bytes 8192 | tf_op jit(solution)/shard_map/all_to_all | solution.py:30
  21.5 23.1 %copy-start = (s32[4,8]{1,0:T(4,128)S(1)}, s32[4,8]{1,0:T(4,128)}, u32[]{:S(2)}) copy-start(s32[4,8]{1,0:T(4,128)} %param.11) | copy-start | bytes 388
  40.3 30.8 %all-to-all-start.3 = ((bf16[8,4,128,128]{3,2,1,0:T(8,128)(2,1)}), bf16[8,4,128,128]{3,2,1,0:T(8,128)(2,1)}, u32[]{:S(2)}, u32[]{:S(2)}) async-start(bf16[8,4,128,128]{3,2,1,0:T(8,128)(2,1)} %bitcast.6), calls=%async_computation.3 | async-start | bytes 2097152 | tf_op jit(solution)/shard_map/all_to_all | solution.py:55
  79.2 25.0 %collective-permute-start = (bf16[2,512,512]{2,1,0:T(8,128)(2,1)}, bf16[2,512,512]{2,1,0:T(8,128)(2,1)}, u32[]{:S(2)}, u32[]{:S(2)}) collective-permute-start(bf16[2,512,512]{2,1,0:T(8,128)(2,1)} %copy.26), channel_id=1, source_target_pairs={{0,3},{1,0},{2,1},{3,2},{4,7},{5,4},{6,5},{7,6},{8,11},{9,8},{10,9... | collective-permute-start | bytes 3145736 | tf_op jit(solution)/shard_map/while/body/eval_jaxpr/ppermute | solution.py:10
  81.3 22.9 %collective-permute-start.1 = (bf16[512,1024]{1,0:T(8,128)(2,1)S(1)}, bf16[512,1024]{1,0:T(8,128)(2,1)}, u32[]{:S(2)}, u32[]{:S(2)}) collective-permute-start(bf16[512,1024]{1,0:T(8,128)(2,1)S(1)} %copy.27), channel_id=1, source_target_pairs={{0,28},{4,0},{8,4},{12,8},{16,12},{20,16},{24,20},{28,24},{1,29},{... | collective-permute-start | bytes 3145736 | tf_op jit(solution)/shard_map/while/body/eval_jaxpr/ppermute | solution.py:10
  106.5 24.2 %collective-permute-start = (bf16[2,512,512]{2,1,0:T(8,128)(2,1)}, bf16[2,512,512]{2,1,0:T(8,128)(2,1)}, u32[]{:S(2)}, u32[]{:S(2)}) collective-permute-start(bf16[2,512,512]{2,1,0:T(8,128)(2,1)} %copy.26), channel_id=1, source_target_pairs={{0,3},{1,0},{2,1},{3,2},{4,7},{5,4},{6,5},{7,6},{8,11},{9,8},{10,9... | collective-permute-start | bytes 3145736 | tf_op jit(solution)/shard_map/while/body/eval_jaxpr/ppermute | solution.py:10
  109.5 21.2 %collective-permute-start.1 = (bf16[512,1024]{1,0:T(8,128)(2,1)S(1)}, bf16[512,1024]{1,0:T(8,128)(2,1)}, u32[]{:S(2)}, u32[]{:S(2)}) collective-permute-start(bf16[512,1024]{1,0:T(8,128)(2,1)S(1)} %copy.27), channel_id=1, source_target_pairs={{0,28},{4,0},{8,4},{12,8},{16,12},{20,16},{24,20},{28,24},{1,29},{... | collective-permute-start | bytes 3145736 | tf_op jit(solution)/shard_map/while/body/eval_jaxpr/ppermute | solution.py:10
  132.9 24.1 %collective-permute-start = (bf16[2,512,512]{2,1,0:T(8,128)(2,1)}, bf16[2,512,512]{2,1,0:T(8,128)(2,1)}, u32[]{:S(2)}, u32[]{:S(2)}) collective-permute-start(bf16[2,512,512]{2,1,0:T(8,128)(2,1)} %copy.26), channel_id=1, source_target_pairs={{0,3},{1,0},{2,1},{3,2},{4,7},{5,4},{6,5},{7,6},{8,11},{9,8},{10,9... | collective-permute-start | bytes 3145736 | tf_op jit(solution)/shard_map/while/body/eval_jaxpr/ppermute | solution.py:10
  136.8 20.2 %collective-permute-start.1 = (bf16[512,1024]{1,0:T(8,128)(2,1)S(1)}, bf16[512,1024]{1,0:T(8,128)(2,1)}, u32[]{:S(2)}, u32[]{:S(2)}) collective-permute-start(bf16[512,1024]{1,0:T(8,128)(2,1)S(1)} %copy.27), channel_id=1, source_target_pairs={{0,28},{4,0},{8,4},{12,8},{16,12},{20,16},{24,20},{28,24},{1,29},{... | collective-permute-start | bytes 3145736 | tf_op jit(solution)/shard_map/while/body/eval_jaxpr/ppermute | solution.py:10
  159.3 23.2 %collective-permute-start = (bf16[2,512,512]{2,1,0:T(8,128)(2,1)}, bf16[2,512,512]{2,1,0:T(8,128)(2,1)}, u32[]{:S(2)}, u32[]{:S(2)}) collective-permute-start(bf16[2,512,512]{2,1,0:T(8,128)(2,1)} %copy.26), channel_id=1, source_target_pairs={{0,3},{1,0},{2,1},{3,2},{4,7},{5,4},{6,5},{7,6},{8,11},{9,8},{10,9... | collective-permute-start | bytes 3145736 | tf_op jit(solution)/shard_map/while/body/eval_jaxpr/ppermute | solution.py:10
  163.2 19.3 %collective-permute-start.1 = (bf16[512,1024]{1,0:T(8,128)(2,1)S(1)}, bf16[512,1024]{1,0:T(8,128)(2,1)}, u32[]{:S(2)}, u32[]{:S(2)}) collective-permute-start(bf16[512,1024]{1,0:T(8,128)(2,1)S(1)} %copy.27), channel_id=1, source_target_pairs={{0,28},{4,0},{8,4},{12,8},{16,12},{20,16},{24,20},{28,24},{1,29},{... | collective-permute-start | bytes 3145736 | tf_op jit(solution)/shard_map/while/body/eval_jaxpr/ppermute | solution.py:10
  184.7 22.3 %collective-permute-start = (bf16[2,512,512]{2,1,0:T(8,128)(2,1)}, bf16[2,512,512]{2,1,0:T(8,128)(2,1)}, u32[]{:S(2)}, u32[]{:S(2)}) collective-permute-start(bf16[2,512,512]{2,1,0:T(8,128)(2,1)} %copy.26), channel_id=1, source_target_pairs={{0,3},{1,0},{2,1},{3,2},{4,7},{5,4},{6,5},{7,6},{8,11},{9,8},{10,9... | collective-permute-start | bytes 3145736 | tf_op jit(solution)/shard_map/while/body/eval_jaxpr/ppermute | solution.py:10
  188.6 18.4 %collective-permute-start.1 = (bf16[512,1024]{1,0:T(8,128)(2,1)S(1)}, bf16[512,1024]{1,0:T(8,128)(2,1)}, u32[]{:S(2)}, u32[]{:S(2)}) collective-permute-start(bf16[512,1024]{1,0:T(8,128)(2,1)S(1)} %copy.27), channel_id=1, source_target_pairs={{0,28},{4,0},{8,4},{12,8},{16,12},{20,16},{24,20},{28,24},{1,29},{... | collective-permute-start | bytes 3145736 | tf_op jit(solution)/shard_map/while/body/eval_jaxpr/ppermute | solution.py:10
  209.3 21.3 %collective-permute-start = (bf16[2,512,512]{2,1,0:T(8,128)(2,1)}, bf16[2,512,512]{2,1,0:T(8,128)(2,1)}, u32[]{:S(2)}, u32[]{:S(2)}) collective-permute-start(bf16[2,512,512]{2,1,0:T(8,128)(2,1)} %copy.26), channel_id=1, source_target_pairs={{0,3},{1,0},{2,1},{3,2},{4,7},{5,4},{6,5},{7,6},{8,11},{9,8},{10,9... | collective-permute-start | bytes 3145736 | tf_op jit(solution)/shard_map/while/body/eval_jaxpr/ppermute | solution.py:10
  213.1 17.5 %collective-permute-start.1 = (bf16[512,1024]{1,0:T(8,128)(2,1)S(1)}, bf16[512,1024]{1,0:T(8,128)(2,1)}, u32[]{:S(2)}, u32[]{:S(2)}) collective-permute-start(bf16[512,1024]{1,0:T(8,128)(2,1)S(1)} %copy.27), channel_id=1, source_target_pairs={{0,28},{4,0},{8,4},{12,8},{16,12},{20,16},{24,20},{28,24},{1,29},{... | collective-permute-start | bytes 3145736 | tf_op jit(solution)/shard_map/while/body/eval_jaxpr/ppermute | solution.py:10
  232.9 21.7 %collective-permute-start = (bf16[2,512,512]{2,1,0:T(8,128)(2,1)}, bf16[2,512,512]{2,1,0:T(8,128)(2,1)}, u32[]{:S(2)}, u32[]{:S(2)}) collective-permute-start(bf16[2,512,512]{2,1,0:T(8,128)(2,1)} %copy.26), channel_id=1, source_target_pairs={{0,3},{1,0},{2,1},{3,2},{4,7},{5,4},{6,5},{7,6},{8,11},{9,8},{10,9... | collective-permute-start | bytes 3145736 | tf_op jit(solution)/shard_map/while/body/eval_jaxpr/ppermute | solution.py:10
  236.7 17.8 %collective-permute-start.1 = (bf16[512,1024]{1,0:T(8,128)(2,1)S(1)}, bf16[512,1024]{1,0:T(8,128)(2,1)}, u32[]{:S(2)}, u32[]{:S(2)}) collective-permute-start(bf16[512,1024]{1,0:T(8,128)(2,1)S(1)} %copy.27), channel_id=1, source_target_pairs={{0,28},{4,0},{8,4},{12,8},{16,12},{20,16},{24,20},{28,24},{1,29},{... | collective-permute-start | bytes 3145736 | tf_op jit(solution)/shard_map/while/body/eval_jaxpr/ppermute | solution.py:10
where the time goes:
time: 260 us; the launch traced here: 258 us
  waiting for transfers between devices  144 us (55%)
  local copies, waits for them, and re-layouts  40.5 us (16%)
  blocking collectives  29.1 us (11%)
  starting transfers between devices  26.2 us (10%)
  matrix products  18 us (7%)
    ppermute x14, waiting for transfers between devices, passed_along(): return lax.ppermute(value, axis, pairs)  122 us
    while x14, local copies, waits for them, and re-layouts  24.4 us
    all_to_all x1, blocking collectives, shards(): lax.all_to_all(a_send, 'col', split_axis=0, concat_axis=0, tiled=True)  18.8 us
    all_to_all x1, waiting for transfers between devices, shards(): lax.all_to_all(b_send, 'row', split_axis=0, concat_axis=0, tiled=True)  18.4 us
    ppermute x14, starting transfers between devices, passed_along(): return lax.ppermute(value, axis, pairs)  16.8 us
    dot_general x7, matrix products, advance(): jnp.dot(a_use, panel_b, preferred_element_type=jnp.float32)  14.4 us
    all_to_all x1, blocking collectives, shards(): lax.all_to_all(b_tags, 'row', split_axis=0, concat_axis=0, tiled=True)  10.3 us
  transfers between devices with their start and end apart: 16, of which 9 were waited for; matrix products, arithmetic and copies ran while one was open for 12% of the time, Pallas kernels for 0%

commit v1 on v0

--- a/solution.py
+++ b/solution.py
@@ -2,6 +2,18 @@
 import jax.numpy as jnp
 from jax import lax
 from jax.sharding import PartitionSpec as P
+
+
+def sent_to_each(x, axis, split, join):
+    ways, here = (lax.axis_size(axis), lax.axis_index(axis))
+    width = x.shape[split] // ways
+    turned = jnp.roll(x, -here * width, axis=split)
+    got = [lax.slice_in_dim(turned, 0, width, axis=split)]
+    for far in range(1, ways):
+        sent = lax.slice_in_dim(turned, far * width, (far + 1) * width, axis=split)
+        got.append(lax.ppermute(sent, axis, [(d, (d + far) % ways) for d in range(ways)]))
+    line = jnp.concatenate(got[::-1], axis=join)
+    return jnp.roll(line, (here + 1) * got[0].shape[join], axis=join)
 
 
 def passed_along(value, axis, steps):
@@ -52,7 +64,7 @@
     b_send = b_blocks.reshape(row_count, -1, block_size, block_size)
     b_tags = b_coord.reshape(row_count, -1, 2)
     b_recv, b_tags = (
-        lax.all_to_all(b_send, "row", split_axis=0, concat_axis=0, tiled=True),
+        sent_to_each(b_send, "row", 0, 0),
         lax.all_to_all(b_tags, "row", split_axis=0, concat_axis=0, tiled=True),
     )
     b_recv = b_recv.reshape(-1, block_size, block_size)

time: 260 us -> 244 us (0.938)
  blocking collectives: 29.1 us -> 0 us
  starting transfers between devices: 26.2 us -> 38.9 us
  waiting for transfers between devices: 144 us -> 134 us
  local copies, waits for them, and re-layouts: 40.5 us -> 45 us
  other arithmetic: 0.05 us -> 4.13 us
    all_to_all x2 -> x0, blocking collectives: 29.1 us -> none  [the longest x1 18.8 us: shards(): lax.all_to_all(a_send, 'col', split_axis=0, concat_axis=0, tiled=True)]
    all_to_all x1 -> x2, waiting for transfers between devices: 18.4 us -> 4.92 us  [the longest x1 4.91 us: shards(): lax.all_to_all(b_tags, 'row', split_axis=0, concat_axis=0, tiled=True)]
    ppermute x0 -> x7, starting transfers between devices: none -> 8.88 us  [sent_to_each(): lax.ppermute(sent, axis, [(d, (d + far) % ways) for d in range(ways)])]
    ppermute x0 -> x7, waiting for transfers between devices: none -> 7.56 us  [sent_to_each(): lax.ppermute(sent, axis, [(d, (d + far) % ways) for d in range(ways)])]
    unnamed x3 -> x16, local copies, waits for them, and re-layouts: 1.29 us -> 5.04 us
    all_to_all x1 -> x2, starting transfers between devices: 4.24 us -> 7.55 us  [the longest x1 4.24 us: shards(): lax.all_to_all(a_send, 'col', split_axis=0, concat_axis=0, tiled=True)]
    concatenate x0 -> x2, other arithmetic: none -> 2.99 us  [the longest x1 1.63 us: sent_to_each(): turned = jnp.roll(x, -here * width, axis=split)]
    ppermute x14, waiting for transfers between devices: 122 us -> 119 us  [passed_along(): return lax.ppermute(value, axis, pairs)]
  transfers between devices with their start and end apart: 16 -> 24, of which waited for: 9 -> 10; matrix products, arithmetic and copies ran while one was open for 12% -> 16% of each run, Pallas kernels for 0% -> 0%
where the time goes in v1:
time: 244 us; the launch traced here: 241 us
  waiting for transfers between devices  134 us (55%)
  local copies, waits for them, and re-layouts  45 us (18%)
  starting transfers between devices  38.9 us (16%)
  matrix products  18.1 us (7%)
  other arithmetic  4.13 us (2%)
    ppermute x14, waiting for transfers between devices, passed_along(): return lax.ppermute(value, axis, pairs)  119 us
    while x14, local copies, waits for them, and re-layouts  24.4 us
    ppermute x14, starting transfers between devices, passed_along(): return lax.ppermute(value, axis, pairs)  18.7 us
    dot_general x7, matrix products, advance(): jnp.dot(a_use, panel_b, preferred_element_type=jnp.float32)  14.5 us
    ppermute x7, starting transfers between devices, sent_to_each(): lax.ppermute(sent, axis, [(d, (d + far) % ways) for d in range(ways)])  8.88 us
    ppermute x7, waiting for transfers between devices, sent_to_each(): lax.ppermute(sent, axis, [(d, (d + far) % ways) for d in range(ways)])  7.56 us
    unnamed x16, local copies, waits for them, and re-layouts  5.04 us
    all_to_all x1, waiting for transfers between devices, shards(): lax.all_to_all(b_tags, 'row', split_axis=0, concat_axis=0, tiled=True)  4.91 us
  transfers between devices with their start and end apart: 24, of which 10 were waited for; matrix products, arithmetic and copies ran while one was open for 16% of the time, Pallas kernels for 0%

profile of v1, /device:TPU:0, one launch (start us, length us, event | category | flops | bytes accessed | tf_op | source)
XLA Modules:
  0.0 240.6 jit_solution(12129100189412566593)
XLA Ops:
  2.5 4.5 %collective-permute-start.2 = (bf16[1,4,128,128]{3,2,1,0:T(8,128)(2,1)}, bf16[1,4,128,128]{3,2,1,0:T(8,128)(2,1)}, u32[]{:S(2)}, u32[]{:S(2)}) collective-permute-start(bf16[1,4,128,128]{3,2,1,0:T(8,128)(2,1)} %get-tuple-element.180), channel_id=1, source_target_pairs={{0,28},{4,0},{8,4},{12,8},{16,12},{20,16},{24,20},{28,24},{1,29},{... | collective-permute-start | bytes 393224 | tf_op jit(solution)/shard_map/ppermute | solution.py:14
  7.5 2.8 %collective-permute-start.5 = (bf16[1,4,128,128]{3,2,1,0:T(8,128)(2,1)}, bf16[1,4,128,128]{3,2,1,0:T(8,128)(2,1)}, u32[]{:S(2)}, u32[]{:S(2)}) collective-permute-start(bf16[1,4,128,128]{3,2,1,0:T(8,128)(2,1)} %get-tuple-element.177), channel_id=1, source_target_pairs={{0,16},{4,20},{8,24},{12,28},{16,0},{20,4},{24,8},{28,12},{1,17},{... | collective-permute-start | bytes 393224 | tf_op jit(solution)/shard_map/ppermute | solution.py:14
  10.9 3.7 %all-to-all-start = ((s32[4,8,2]{1,2,0:T(2,128)}), s32[4,8,2]{1,2,0:T(2,128)S(1)}, u32[]{:S(2)}, u32[]{:S(2)}) async-start(s32[4,8,2]{1,2,0:T(2,128)} %copy.8), calls=%async_computation | async-start | bytes 8192 | tf_op jit(solution)/shard_map/all_to_all | solution.py:42
  16.6 2.7 %all-to-all-done = s32[4,8,2]{1,2,0:T(2,128)S(1)} async-done(((s32[4,8,2]{1,2,0:T(2,128)}), s32[4,8,2]{1,2,0:T(2,128)S(1)}, u32[]{:S(2)}, u32[]{:S(2)}) %all-to-all-start) | async-done | bytes 288 | tf_op jit(solution)/shard_map/all_to_all | solution.py:42
  19.3 3.3 %all-to-all-start.2 = ((s32[8,4,2]{1,2,0:T(2,128)}), s32[8,4,2]{1,2,0:T(2,128)S(1)}, u32[]{:S(2)}, u32[]{:S(2)}) async-start(s32[8,4,2]{1,2,0:T(2,128)} %copy.11), calls=%async_computation.2 | async-start | bytes 16384 | tf_op jit(solution)/shard_map/all_to_all | solution.py:68
  23.3 4.9 %all-to-all-done.2 = s32[8,4,2]{1,2,0:T(2,128)S(1)} async-done(((s32[8,4,2]{1,2,0:T(2,128)}), s32[8,4,2]{1,2,0:T(2,128)S(1)}, u32[]{:S(2)}, u32[]{:S(2)}) %all-to-all-start.2) | async-done | bytes 288 | tf_op jit(solution)/shard_map/all_to_all | solution.py:68
  28.2 4.2 %all-to-all-start.1 = ((bf16[4,8,128,128]{3,2,1,0:T(8,128)(2,1)}), bf16[4,8,128,128]{3,2,1,0:T(8,128)(2,1)}, u32[]{:S(2)}, u32[]{:S(2)}) async-start(bf16[4,8,128,128]{3,2,1,0:T(8,128)(2,1)} %bitcast.49), calls=%async_computation.1 | async-start | bytes 2097152 | tf_op jit(solution)/shard_map/all_to_all | solution.py:41
  37.4 7.5 %collective-permute-done.6 = bf16[1,4,128,128]{3,2,1,0:T(8,128)(2,1)S(1)} collective-permute-done((bf16[1,4,128,128]{3,2,1,0:T(8,128)(2,1)S(1)}, bf16[1,4,128,128]{3,2,1,0:T(8,128)(2,1)S(1)}, u32[]{:S(2)}, u32[]{:S(2)}) %collective-permute-start.6) | collective-permute-done | bytes 131104 | tf_op jit(solution)/shard_map/ppermute | solution.py:14
  46.6 3.6 %scatter_fusion.1 = bf16[32,128,128]{2,1,0:T(8,128)(2,1)S(1)} fusion(bf16[32,128,128]{2,1,0:T(8,128)(2,1)S(1)} %broadcast.70.clone.1, s32[32]{0:T(128)S(1)} %fusion.13, bf16[32,128,128]{2,1,0:T(8,128)(2,1)} %bitcast.46), kind=kCustom, calls=%fused_computation.1 | custom fusion | bytes 3145856 | tf_op jit(solution)/shard_map/scatter | solution.py:79
  52.4 3.6 %scatter_fusion = bf16[32,128,128]{2,1,0:T(8,128)(2,1)S(1)} fusion(bf16[32,128,128]{2,1,0:T(8,128)(2,1)S(1)} %broadcast.70.clone, s32[32]{0:T(128)S(1)} %copy-done.2, bf16[32,128,128]{2,1,0:T(8,128)(2,1)} %bitcast.2), kind=kCustom, calls=%fused_computation | custom fusion | bytes 3145856 | tf_op jit(solution)/shard_map/scatter | solution.py:58
  60.1 176.7 %while.20 = (s32[]{:T(128)}, bf16[2,512,512]{2,1,0:T(8,128)(2,1)}, bf16[512,1024]{1,0:T(8,128)(2,1)}, f32[512,1024]{1,0:T(8,128)S(1)}, s32[]{:T(128)}, /*index=5...) while((s32[]{:T(128)}, bf16[2,512,512]{2,1,0:T(8,128)(2,1)}, ...), condition=%wide.region_3.5_spmd.clone, body=%wide.region_2.4_spmd.clone.sunk | while | flops 537919488 | bytes 18350596 | solution.py:94
  62.3 2.9 %collective-permute-start = (bf16[2,512,512]{2,1,0:T(8,128)(2,1)}, bf16[2,512,512]{2,1,0:T(8,128)(2,1)}, u32[]{:S(2)}, u32[]{:S(2)}) collective-permute-start(bf16[2,512,512]{2,1,0:T(8,128)(2,1)} %copy.33), channel_id=1, source_target_pairs={{0,3},{1,0},{2,1},{3,2},{4,7},{5,4},{6,5},{7,6},{8,11},{9,8},{10,9... | collective-permute-start | bytes 3145736 | tf_op jit(solution)/shard_map/while/body/eval_jaxpr/ppermute | solution.py:22
  68.5 16.4 %collective-permute-done = bf16[2,512,512]{2,1,0:T(8,128)(2,1)} collective-permute-done((bf16[2,512,512]{2,1,0:T(8,128)(2,1)}, bf16[2,512,512]{2,1,0:T(8,128)(2,1)}, u32[]{:S(2)}, u32[]{:S(2)}) %collective-permute-start) | collective-permute-done | bytes 1048608 | tf_op jit(solution)/shard_map/while/body/eval_jaxpr/ppermute | solution.py:22
  87.2 3.4 %collective-permute-start = (bf16[2,512,512]{2,1,0:T(8,128)(2,1)}, bf16[2,512,512]{2,1,0:T(8,128)(2,1)}, u32[]{:S(2)}, u32[]{:S(2)}) collective-permute-start(bf16[2,512,512]{2,1,0:T(8,128)(2,1)} %copy.33), channel_id=1, source_target_pairs={{0,3},{1,0},{2,1},{3,2},{4,7},{5,4},{6,5},{7,6},{8,11},{9,8},{10,9... | collective-permute-start | bytes 3145736 | tf_op jit(solution)/shard_map/while/body/eval_jaxpr/ppermute | solution.py:22
  93.9 15.5 %collective-permute-done = bf16[2,512,512]{2,1,0:T(8,128)(2,1)} collective-permute-done((bf16[2,512,512]{2,1,0:T(8,128)(2,1)}, bf16[2,512,512]{2,1,0:T(8,128)(2,1)}, u32[]{:S(2)}, u32[]{:S(2)}) %collective-permute-start) | collective-permute-done | bytes 1048608 | tf_op jit(solution)/shard_map/while/body/eval_jaxpr/ppermute | solution.py:22
  111.7 3.4 %collective-permute-start = (bf16[2,512,512]{2,1,0:T(8,128)(2,1)}, bf16[2,512,512]{2,1,0:T(8,128)(2,1)}, u32[]{:S(2)}, u32[]{:S(2)}) collective-permute-start(bf16[2,512,512]{2,1,0:T(8,128)(2,1)} %copy.33), channel_id=1, source_target_pairs={{0,3},{1,0},{2,1},{3,2},{4,7},{5,4},{6,5},{7,6},{8,11},{9,8},{10,9... | collective-permute-start | bytes 3145736 | tf_op jit(solution)/shard_map/while/body/eval_jaxpr/ppermute | solution.py:22
  118.8 14.6 %collective-permute-done = bf16[2,512,512]{2,1,0:T(8,128)(2,1)} collective-permute-done((bf16[2,512,512]{2,1,0:T(8,128)(2,1)}, bf16[2,512,512]{2,1,0:T(8,128)(2,1)}, u32[]{:S(2)}, u32[]{:S(2)}) %collective-permute-start) | collective-permute-done | bytes 1048608 | tf_op jit(solution)/shard_map/while/body/eval_jaxpr/ppermute | solution.py:22
  133.4 2.3 copy.33
  135.7 2.9 %collective-permute-start = (bf16[2,512,512]{2,1,0:T(8,128)(2,1)}, bf16[2,512,512]{2,1,0:T(8,128)(2,1)}, u32[]{:S(2)}, u32[]{:S(2)}) collective-permute-start(bf16[2,512,512]{2,1,0:T(8,128)(2,1)} %copy.33), channel_id=1, source_target_pairs={{0,3},{1,0},{2,1},{3,2},{4,7},{5,4},{6,5},{7,6},{8,11},{9,8},{10,9... | collective-permute-start | bytes 3145736 | tf_op jit(solution)/shard_map/while/body/eval_jaxpr/ppermute | solution.py:22
  143.7 16.9 %collective-permute-done = bf16[2,512,512]{2,1,0:T(8,128)(2,1)} collective-permute-done((bf16[2,512,512]{2,1,0:T(8,128)(2,1)}, bf16[2,512,512]{2,1,0:T(8,128)(2,1)}, u32[]{:S(2)}, u32[]{:S(2)}) %collective-permute-start) | collective-permute-done | bytes 1048608 | tf_op jit(solution)/shard_map/while/body/eval_jaxpr/ppermute | solution.py:22
  167.7 19.2 %collective-permute-done = bf16[2,512,512]{2,1,0:T(8,128)(2,1)} collective-permute-done((bf16[2,512,512]{2,1,0:T(8,128)(2,1)}, bf16[2,512,512]{2,1,0:T(8,128)(2,1)}, u32[]{:S(2)}, u32[]{:S(2)}) %collective-permute-start) | collective-permute-done | bytes 1048608 | tf_op jit(solution)/shard_map/while/body/eval_jaxpr/ppermute | solution.py:22
  193.7 18.6 %collective-permute-done = bf16[2,512,512]{2,1,0:T(8,128)(2,1)} collective-permute-done((bf16[2,512,512]{2,1,0:T(8,128)(2,1)}, bf16[2,512,512]{2,1,0:T(8,128)(2,1)}, u32[]{:S(2)}, u32[]{:S(2)}) %collective-permute-start) | collective-permute-done | bytes 1048608 | tf_op jit(solution)/shard_map/while/body/eval_jaxpr/ppermute | solution.py:22
  219.1 17.7 %collective-permute-done = bf16[2,512,512]{2,1,0:T(8,128)(2,1)} collective-permute-done((bf16[2,512,512]{2,1,0:T(8,128)(2,1)}, bf16[2,512,512]{2,1,0:T(8,128)(2,1)}, u32[]{:S(2)}, u32[]{:S(2)}) %collective-permute-start) | collective-permute-done | bytes 1048608 | tf_op jit(solution)/shard_map/while/body/eval_jaxpr/ppermute | solution.py:22
  237.0 3.6 %bitcast_multiply_fusion = f32[512,1024]{1,0:T(8,128)} fusion(f32[64,8,8,128]{3,2,1,0:T(8,128)S(1)} %bitcast.45, f32[512,1024]{1,0:T(8,128)S(1)} %get-tuple-element.143, bf16[512,1024]{1,0:T(8,128)(2,1)} %get-tuple-element.145, bf16[2,512,512]{2,1,0:T(8,128)(2,1)} %get-tuple-element.144, s32[]{:T(128)S(6)} %select_n.110), kind=kOutput, calls=%fused_computation.6 | convolution fusion | flops 537919488 | bytes 7864324 | tf_op jit(solution)/shard_map/dot_general | solution.py:99
  (87 shorter events, 62.1 us)
Async XLA Ops:
  2.5 30.2 %collective-permute-start.2 = (bf16[1,4,128,128]{3,2,1,0:T(8,128)(2,1)}, bf16[1,4,128,128]{3,2,1,0:T(8,128)(2,1)}, u32[]{:S(2)}, u32[]{:S(2)}) collective-permute-start(bf16[1,4,128,128]{3,2,1,0:T(8,128)(2,1)} %get-tuple-element.180), channel_id=1, source_target_pairs={{0,28},{4,0},{8,4},{12,8},{16,12},{20,16},{24,20},{28,24},{1,29},{... | collective-permute-start | bytes 393224 | tf_op jit(solution)/shard_map/ppermute | solution.py:14
  7.0 27.2 %collective-permute-start.3 = (bf16[1,4,128,128]{3,2,1,0:T(8,128)(2,1)}, bf16[1,4,128,128]{3,2,1,0:T(8,128)(2,1)}, u32[]{:S(2)}, u32[]{:S(2)}) collective-permute-start(bf16[1,4,128,128]{3,2,1,0:T(8,128)(2,1)} %get-tuple-element.179), channel_id=1, source_target_pairs={{0,24},{4,28},{8,0},{12,4},{16,8},{20,12},{24,16},{28,20},{1,25},{... | collective-permute-start | bytes 393224 | tf_op jit(solution)/shard_map/ppermute | solution.py:14
  7.5 28.0 %collective-permute-start.4 = (bf16[1,4,128,128]{3,2,1,0:T(8,128)(2,1)}, bf16[1,4,128,128]{3,2,1,0:T(8,128)(2,1)}, u32[]{:S(2)}, u32[]{:S(2)}) collective-permute-start(bf16[1,4,128,128]{3,2,1,0:T(8,128)(2,1)} %get-tuple-element.178), channel_id=1, source_target_pairs={{0,20},{4,24},{8,28},{12,0},{16,4},{20,8},{24,12},{28,16},{1,21},{... | collective-permute-start | bytes 393224 | tf_op jit(solution)/shard_map/ppermute | solution.py:14
  7.5 28.9 %collective-permute-start.5 = (bf16[1,4,128,128]{3,2,1,0:T(8,128)(2,1)}, bf16[1,4,128,128]{3,2,1,0:T(8,128)(2,1)}, u32[]{:S(2)}, u32[]{:S(2)}) collective-permute-start(bf16[1,4,128,128]{3,2,1,0:T(8,128)(2,1)} %get-tuple-element.177), channel_id=1, source_target_pairs={{0,16},{4,20},{8,24},{12,28},{16,0},{20,4},{24,8},{28,12},{1,17},{... | collective-permute-start | bytes 393224 | tf_op jit(solution)/shard_map/ppermute | solution.py:14
  10.9 8.4 %all-to-all-start = ((s32[4,8,2]{1,2,0:T(2,128)}), s32[4,8,2]{1,2,0:T(2,128)S(1)}, u32[]{:S(2)}, u32[]{:S(2)}) async-start(s32[4,8,2]{1,2,0:T(2,128)} %copy.8), calls=%async_computation | async-start | bytes 8192 | tf_op jit(solution)/shard_map/all_to_all | solution.py:42
  19.3 8.9 %all-to-all-start.2 = ((s32[8,4,2]{1,2,0:T(2,128)}), s32[8,4,2]{1,2,0:T(2,128)S(1)}, u32[]{:S(2)}, u32[]{:S(2)}) async-start(s32[8,4,2]{1,2,0:T(2,128)} %copy.11), calls=%async_computation.2 | async-start | bytes 16384 | tf_op jit(solution)/shard_map/all_to_all | solution.py:68
  28.2 24.0 %all-to-all-start.1 = ((bf16[4,8,128,128]{3,2,1,0:T(8,128)(2,1)}), bf16[4,8,128,128]{3,2,1,0:T(8,128)(2,1)}, u32[]{:S(2)}, u32[]{:S(2)}) async-start(bf16[4,8,128,128]{3,2,1,0:T(8,128)(2,1)} %bitcast.49), calls=%async_computation.1 | async-start | bytes 2097152 | tf_op jit(solution)/shard_map/all_to_all | solution.py:41
  32.5 12.4 %collective-permute-start.6 = (bf16[1,4,128,128]{3,2,1,0:T(8,128)(2,1)S(1)}, bf16[1,4,128,128]{3,2,1,0:T(8,128)(2,1)S(1)}, u32[]{:S(2)}, u32[]{:S(2)}) collective-permute-start(bf16[1,4,128,128]{3,2,1,0:T(8,128)(2,1)S(1)} %get-tuple-element.176), channel_id=1, source_target_pairs={{0,12},{4,16},{8,20},{12,24},{16,28},{20,0},{24,4},{28,8},{1,13},{... | collective-permute-start | bytes 393224 | tf_op jit(solution)/shard_map/ppermute | solution.py:14
  33.5 11.4 %collective-permute-start.7 = (bf16[1,4,128,128]{3,2,1,0:T(8,128)(2,1)S(1)}, bf16[1,4,128,128]{3,2,1,0:T(8,128)(2,1)S(1)}, u32[]{:S(2)}, u32[]{:S(2)}) collective-permute-start(bf16[1,4,128,128]{3,2,1,0:T(8,128)(2,1)S(1)} %get-tuple-element.175), channel_id=1, source_target_pairs={{0,8},{4,12},{8,16},{12,20},{16,24},{20,28},{24,0},{28,4},{1,9},{5... | collective-permute-start | bytes 393224 | tf_op jit(solution)/shard_map/ppermute | solution.py:14
  35.1 9.9 %collective-permute-start.8 = (bf16[1,4,128,128]{3,2,1,0:T(8,128)(2,1)S(1)}, bf16[1,4,128,128]{3,2,1,0:T(8,128)(2,1)S(1)}, u32[]{:S(2)}, u32[]{:S(2)}) collective-permute-start(bf16[1,4,128,128]{3,2,1,0:T(8,128)(2,1)S(1)} %get-tuple-element.174), channel_id=1, source_target_pairs={{0,4},{4,8},{8,12},{12,16},{16,20},{20,24},{24,28},{28,0},{1,5},{5... | collective-permute-start | bytes 393224 | tf_op jit(solution)/shard_map/ppermute | solution.py:14
  62.3 22.6 %collective-permute-start = (bf16[2,512,512]{2,1,0:T(8,128)(2,1)}, bf16[2,512,512]{2,1,0:T(8,128)(2,1)}, u32[]{:S(2)}, u32[]{:S(2)}) collective-permute-start(bf16[2,512,512]{2,1,0:T(8,128)(2,1)} %copy.33), channel_id=1, source_target_pairs={{0,3},{1,0},{2,1},{3,2},{4,7},{5,4},{6,5},{7,6},{8,11},{9,8},{10,9... | collective-permute-start | bytes 3145736 | tf_op jit(solution)/shard_map/while/body/eval_jaxpr/ppermute | solution.py:22
  66.5 18.5 %collective-permute-start.1 = (bf16[512,1024]{1,0:T(8,128)(2,1)S(1)}, bf16[512,1024]{1,0:T(8,128)(2,1)}, u32[]{:S(2)}, u32[]{:S(2)}) collective-permute-start(bf16[512,1024]{1,0:T(8,128)(2,1)S(1)} %copy.34), channel_id=1, source_target_pairs={{0,28},{4,0},{8,4},{12,8},{16,12},{20,16},{24,20},{28,24},{1,29},{... | collective-permute-start | bytes 3145736 | tf_op jit(solution)/shard_map/while/body/eval_jaxpr/ppermute | solution.py:22
  87.2 22.2 %collective-permute-start = (bf16[2,512,512]{2,1,0:T(8,128)(2,1)}, bf16[2,512,512]{2,1,0:T(8,128)(2,1)}, u32[]{:S(2)}, u32[]{:S(2)}) collective-permute-start(bf16[2,512,512]{2,1,0:T(8,128)(2,1)} %copy.33), channel_id=1, source_target_pairs={{0,3},{1,0},{2,1},{3,2},{4,7},{5,4},{6,5},{7,6},{8,11},{9,8},{10,9... | collective-permute-start | bytes 3145736 | tf_op jit(solution)/shard_map/while/body/eval_jaxpr/ppermute | solution.py:22
  91.8 17.6 %collective-permute-start.1 = (bf16[512,1024]{1,0:T(8,128)(2,1)S(1)}, bf16[512,1024]{1,0:T(8,128)(2,1)}, u32[]{:S(2)}, u32[]{:S(2)}) collective-permute-start(bf16[512,1024]{1,0:T(8,128)(2,1)S(1)} %copy.34), channel_id=1, source_target_pairs={{0,28},{4,0},{8,4},{12,8},{16,12},{20,16},{24,20},{28,24},{1,29},{... | collective-permute-start | bytes 3145736 | tf_op jit(solution)/shard_map/while/body/eval_jaxpr/ppermute | solution.py:22
  111.7 21.7 %collective-permute-start = (bf16[2,512,512]{2,1,0:T(8,128)(2,1)}, bf16[2,512,512]{2,1,0:T(8,128)(2,1)}, u32[]{:S(2)}, u32[]{:S(2)}) collective-permute-start(bf16[2,512,512]{2,1,0:T(8,128)(2,1)} %copy.33), channel_id=1, source_target_pairs={{0,3},{1,0},{2,1},{3,2},{4,7},{5,4},{6,5},{7,6},{8,11},{9,8},{10,9... | collective-permute-start | bytes 3145736 | tf_op jit(solution)/shard_map/while/body/eval_jaxpr/ppermute | solution.py:22
  116.3 17.1 %collective-permute-start.1 = (bf16[512,1024]{1,0:T(8,128)(2,1)S(1)}, bf16[512,1024]{1,0:T(8,128)(2,1)}, u32[]{:S(2)}, u32[]{:S(2)}) collective-permute-start(bf16[512,1024]{1,0:T(8,128)(2,1)S(1)} %copy.34), channel_id=1, source_target_pairs={{0,28},{4,0},{8,4},{12,8},{16,12},{20,16},{24,20},{28,24},{1,29},{... | collective-permute-start | bytes 3145736 | tf_op jit(solution)/shard_map/while/body/eval_jaxpr/ppermute | solution.py:22
  135.7 25.0 %collective-permute-start = (bf16[2,512,512]{2,1,0:T(8,128)(2,1)}, bf16[2,512,512]{2,1,0:T(8,128)(2,1)}, u32[]{:S(2)}, u32[]{:S(2)}) collective-permute-start(bf16[2,512,512]{2,1,0:T(8,128)(2,1)} %copy.33), channel_id=1, source_target_pairs={{0,3},{1,0},{2,1},{3,2},{4,7},{5,4},{6,5},{7,6},{8,11},{9,8},{10,9... | collective-permute-start | bytes 3145736 | tf_op jit(solution)/shard_map/while/body/eval_jaxpr/ppermute | solution.py:22
  139.8 20.8 %collective-permute-start.1 = (bf16[512,1024]{1,0:T(8,128)(2,1)S(1)}, bf16[512,1024]{1,0:T(8,128)(2,1)}, u32[]{:S(2)}, u32[]{:S(2)}) collective-permute-start(bf16[512,1024]{1,0:T(8,128)(2,1)S(1)} %copy.34), channel_id=1, source_target_pairs={{0,28},{4,0},{8,4},{12,8},{16,12},{20,16},{24,20},{28,24},{1,29},{... | collective-permute-start | bytes 3145736 | tf_op jit(solution)/shard_map/while/body/eval_jaxpr/ppermute | solution.py:22
  162.9 24.0 %collective-permute-start = (bf16[2,512,512]{2,1,0:T(8,128)(2,1)}, bf16[2,512,512]{2,1,0:T(8,128)(2,1)}, u32[]{:S(2)}, u32[]{:S(2)}) collective-permute-start(bf16[2,512,512]{2,1,0:T(8,128)(2,1)} %copy.33), channel_id=1, source_target_pairs={{0,3},{1,0},{2,1},{3,2},{4,7},{5,4},{6,5},{7,6},{8,11},{9,8},{10,9... | collective-permute-start | bytes 3145736 | tf_op jit(solution)/shard_map/while/body/eval_jaxpr/ppermute | solution.py:22
  165.3 21.6 %collective-permute-start.1 = (bf16[512,1024]{1,0:T(8,128)(2,1)S(1)}, bf16[512,1024]{1,0:T(8,128)(2,1)}, u32[]{:S(2)}, u32[]{:S(2)}) collective-permute-start(bf16[512,1024]{1,0:T(8,128)(2,1)S(1)} %copy.34), channel_id=1, source_target_pairs={{0,28},{4,0},{8,4},{12,8},{16,12},{20,16},{24,20},{28,24},{1,29},{... | collective-permute-start | bytes 3145736 | tf_op jit(solution)/shard_map/while/body/eval_jaxpr/ppermute | solution.py:22
  189.2 23.1 %collective-permute-start = (bf16[2,512,512]{2,1,0:T(8,128)(2,1)}, bf16[2,512,512]{2,1,0:T(8,128)(2,1)}, u32[]{:S(2)}, u32[]{:S(2)}) collective-permute-start(bf16[2,512,512]{2,1,0:T(8,128)(2,1)} %copy.33), channel_id=1, source_target_pairs={{0,3},{1,0},{2,1},{3,2},{4,7},{5,4},{6,5},{7,6},{8,11},{9,8},{10,9... | collective-permute-start | bytes 3145736 | tf_op jit(solution)/shard_map/while/body/eval_jaxpr/ppermute | solution.py:22
  191.6 20.7 %collective-permute-start.1 = (bf16[512,1024]{1,0:T(8,128)(2,1)S(1)}, bf16[512,1024]{1,0:T(8,128)(2,1)}, u32[]{:S(2)}, u32[]{:S(2)}) collective-permute-start(bf16[512,1024]{1,0:T(8,128)(2,1)S(1)} %copy.34), channel_id=1, source_target_pairs={{0,28},{4,0},{8,4},{12,8},{16,12},{20,16},{24,20},{28,24},{1,29},{... | collective-permute-start | bytes 3145736 | tf_op jit(solution)/shard_map/while/body/eval_jaxpr/ppermute | solution.py:22
  214.6 22.2 %collective-permute-start = (bf16[2,512,512]{2,1,0:T(8,128)(2,1)}, bf16[2,512,512]{2,1,0:T(8,128)(2,1)}, u32[]{:S(2)}, u32[]{:S(2)}) collective-permute-start(bf16[2,512,512]{2,1,0:T(8,128)(2,1)} %copy.33), channel_id=1, source_target_pairs={{0,3},{1,0},{2,1},{3,2},{4,7},{5,4},{6,5},{7,6},{8,11},{9,8},{10,9... | collective-permute-start | bytes 3145736 | tf_op jit(solution)/shard_map/while/body/eval_jaxpr/ppermute | solution.py:22
  217.0 19.8 %collective-permute-start.1 = (bf16[512,1024]{1,0:T(8,128)(2,1)S(1)}, bf16[512,1024]{1,0:T(8,128)(2,1)}, u32[]{:S(2)}, u32[]{:S(2)}) collective-permute-start(bf16[512,1024]{1,0:T(8,128)(2,1)S(1)} %copy.34), channel_id=1, source_target_pairs={{0,28},{4,0},{8,4},{12,8},{16,12},{20,16},{24,20},{28,24},{1,29},{... | collective-permute-start | bytes 3145736 | tf_op jit(solution)/shard_map/while/body/eval_jaxpr/ppermute | solution.py:22
  (4 other events, 204.5 us)
